TPU v7x, 32 devices: a whole 2x2x4 slice. The times are simulated.
32 devices in a mesh: dp: 4 (over y, x), expert: 8 (over z, core).
Axes of the slice: x: 2, y: 2, z: 4, core: 2. Of those that a mesh axis runs over, the one named last changes fastest.
Arguments:
- tokens: bfloat16 [4096, 2048], P(('dp', 'expert')), may hold values from -6 to 6
- cotangent: bfloat16 [4096, 2048], P(('dp', 'expert')), may hold values from -6 to 6
- routes: int32 [4096, 2], P(('dp', 'expert')), may hold values from 0 to 7, as said below
- route_weights: float32 [4096, 2], P(('dp', 'expert')), may hold values from 0.1 to 1
- capacity: int32 [8], replicated, may hold values from 16 to 32, as said below
- w_in: bfloat16 [8, 2, 1408, 2048], P('expert', None, 'dp'), may hold values from -0.125 to 0.125
- w_down: bfloat16 [8, 1408, 2048], P('expert', 'dp'), may hold values from -0.15625 to 0.15625
Outputs:
- mixed: bfloat16 [4096, 2048], P(('dp', 'expert'))
- d_tokens: bfloat16 [4096, 2048], P(('dp', 'expert'))
- d_route_weights: float32 [4096, 2], P(('dp', 'expert'))
- d_w_in: bfloat16 [8, 2, 1408, 2048], P('expert', None, 'dp')
- d_w_down: bfloat16 [8, 1408, 2048], P('expert', 'dp')
Inputs may be any that keep to these rules, and one draw needn't show every extreme that they name: Each token names two different experts; in every block of 128 rows (one device's tokens) some expert whose capacity is 32 is named by 32 or more routes. Some expert has capacity 32.
All inputs are finite; a program needn't handle non-finite values.
Results may differ from a plain program's by a relative error of at most 0.013.
Values may be sent and summed in bfloat16 or wider, within the bound.
A program may use at most 128 MiB of HBM per device.

v0:
```python
import jax
import jax.numpy as jnp
from jax import lax
from jax.sharding import PartitionSpec as P


def expert_forward(inputs, weights_in, weights_down):
    gate_value = jnp.einsum(
        "gecd,ehd->gech", inputs, weights_in[:, 0], preferred_element_type=jnp.float32
    )
    up_value = jnp.einsum(
        "gecd,ehd->gech", inputs, weights_in[:, 1], preferred_element_type=jnp.float32
    )
    sig_gate = jax.nn.sigmoid(gate_value)
    act_gate = gate_value * sig_gate
    hidden = (act_gate * up_value).astype(jnp.bfloat16)
    partial_out = jnp.einsum(
        "gech,ehd->gecd", hidden, weights_down, preferred_element_type=jnp.float32
    )
    return ((gate_value, up_value, sig_gate, act_gate, hidden), partial_out)


def expert_backward(inputs, scaled, weights_in, weights_down, saved):
    gate_value, up_value, sig_gate, act_gate, hidden = saved
    hidden_grad = jnp.einsum(
        "gecd,ehd->gech", scaled, weights_down, preferred_element_type=jnp.float32
    )
    slope_gate = sig_gate * (1.0 + gate_value * (1.0 - sig_gate))
    gate_grad = (hidden_grad * up_value * slope_gate).astype(jnp.bfloat16)
    up_grad = (hidden_grad * act_gate).astype(jnp.bfloat16)
    gate_weight_grad = jnp.einsum(
        "gech,gecd->ehd", gate_grad, inputs, preferred_element_type=jnp.float32
    )
    up_weight_grad = jnp.einsum(
        "gech,gecd->ehd", up_grad, inputs, preferred_element_type=jnp.float32
    )
    down_weight_grad = jnp.einsum(
        "gech,gecd->ehd", hidden, scaled, preferred_element_type=jnp.float32
    )
    input_grad = jnp.einsum(
        "gech,ehd->gecd", gate_grad, weights_in[:, 0], preferred_element_type=jnp.float32
    )
    input_grad = input_grad + jnp.einsum(
        "gech,ehd->gecd", up_grad, weights_in[:, 1], preferred_element_type=jnp.float32
    )
    return (jnp.stack([gate_weight_grad, up_weight_grad], axis=1), down_weight_grad, input_grad)


def body(tokens, cotangent, routes, route_weights, capacity, w_in, w_down):
    experts = capacity.shape[0]
    expert_devs = lax.axis_size("expert")
    local_experts = experts // expert_devs
    tok_rows = tokens.shape[0]
    width = tokens.shape[1]
    slots = tok_rows * 2 // experts
    flat_expert = routes.reshape(-1)
    expert_ids = jnp.arange(experts, dtype=jnp.int32)
    onehot = (flat_expert[:, None] == expert_ids[None, :]).astype(jnp.int32)
    earlier = jnp.cumsum(onehot, axis=0) - onehot
    route_rank = jnp.sum(earlier * onehot, axis=1)
    cap_limit = jnp.sum(onehot * capacity[None, :], axis=1)
    kept_mask = route_rank < cap_limit
    dummy = experts * slots
    slot_target = jnp.where(kept_mask, flat_expert * slots + route_rank, dummy)
    route_count = 2 * tok_rows
    route_ids = jnp.arange(route_count, dtype=jnp.int32)
    slot_owner = (
        jnp.full((dummy + 1,), route_count, jnp.int32).at[slot_target].set(route_ids)[:dummy]
    )
    token_of = slot_owner // 2
    padded_tokens = jnp.concatenate([tokens, jnp.zeros((1, width), tokens.dtype)], axis=0)
    padded_cot = jnp.concatenate([cotangent, jnp.zeros((1, width), cotangent.dtype)], axis=0)
    padded_weights = jnp.concatenate(
        [route_weights.reshape(-1), jnp.zeros((1,), jnp.float32)], axis=0
    )
    bucket_shape = (expert_devs, local_experts, slots, width)
    send_inputs = padded_tokens[token_of].reshape(bucket_shape)
    send_scaled = (
        (padded_weights[slot_owner][:, None] * padded_cot[token_of].astype(jnp.float32))
        .astype(jnp.bfloat16)
        .reshape(bucket_shape)
    )
    recv_inputs = lax.all_to_all(send_inputs, "expert", split_axis=0, concat_axis=0, tiled=True)
    use_inputs = lax.all_gather(recv_inputs, "dp", axis=0, tiled=True)
    saved, partial_out = expert_forward(use_inputs, w_in, w_down)
    out_local = lax.psum_scatter(
        partial_out.astype(jnp.bfloat16), "dp", scatter_dimension=0, tiled=True
    )
    out_back = lax.all_to_all(out_local, "expert", split_axis=0, concat_axis=0, tiled=True)
    recv_scaled = lax.all_to_all(send_scaled, "expert", split_axis=0, concat_axis=0, tiled=True)
    use_scaled = lax.all_gather(recv_scaled, "dp", axis=0, tiled=True)
    in_weight_grad, down_weight_grad, input_grad = expert_backward(
        use_inputs, use_scaled, w_in, w_down, saved
    )
    grad_local = lax.psum_scatter(
        input_grad.astype(jnp.bfloat16), "dp", scatter_dimension=0, tiled=True
    )
    grad_back = lax.all_to_all(grad_local, "expert", split_axis=0, concat_axis=0, tiled=True)
    flat_out = jnp.concatenate(
        [out_back.reshape(dummy, width), jnp.zeros((1, width), jnp.bfloat16)], axis=0
    )
    flat_grad = jnp.concatenate(
        [grad_back.reshape(dummy, width), jnp.zeros((1, width), jnp.bfloat16)], axis=0
    )
    out_route = flat_out[slot_target].reshape(tok_rows, 2, width).astype(jnp.float32)
    grad_route = flat_grad[slot_target].reshape(tok_rows, 2, width).astype(jnp.float32)
    mixed = jnp.sum(route_weights[:, :, None] * out_route, axis=1).astype(jnp.bfloat16)
    d_route_weights = jnp.sum(out_route * cotangent.astype(jnp.float32)[:, None, :], axis=2)
    d_tokens = jnp.sum(grad_route, axis=1).astype(jnp.bfloat16)
    return (
        mixed,
        d_tokens,
        d_route_weights,
        in_weight_grad.astype(jnp.bfloat16),
        down_weight_grad.astype(jnp.bfloat16),
    )


def solution(mesh):
    placed = (
        P(("dp", "expert"), None),
        P(("dp", "expert"), None),
        P(("dp", "expert"), None),
        P(("dp", "expert"), None),
        P(),
        P("expert", None, "dp", None),
        P("expert", "dp", None),
    )
    return jax.shard_map(
        body,
        mesh=mesh,
        in_specs=placed,
        out_specs=(
            P(("dp", "expert"), None),
            P(("dp", "expert"), None),
            P(("dp", "expert"), None),
            P("expert", None, "dp", None),
            P("expert", "dp", None),
        ),
        check_vma=False,
    )
```

profile of v0, /device:TPU:0, one launch (start us, length us, event | category | flops | bytes accessed | tf_op | source)
XLA Modules:
  0.0 320.7 jit_solution(16261280849117789705)
XLA Ops:
  11.0 1.4 scatter_custom_fusion
  13.5 1.4 gather_fusion
  14.9 32.8 %all_to_all.20 = bf16[8,1,32,2048]{3,2,1,0:T(8,128)(2,1)} all-to-all(bf16[8,1,32,2048]{3,2,1,0:T(8,128)(2,1)S(1)} %bitcast.184), channel_id=1, replica_groups=mesh['dp'=4,'expert'=8] {'expert'}, dimensions={0} | all-to-all | bytes 2097152 | tf_op jit(solution)/shard_map/all_to_all | solution.py:83
  48.1 1.9 gather_fusion.2
  50.1 1.4 gather_fusion.3
  51.8 29.7 %all_to_all.21 = bf16[8,1,32,2048]{3,2,1,0:T(8,128)(2,1)} all-to-all(bf16[8,1,32,2048]{3,2,1,0:T(8,128)(2,1)S(1)} %fusion.40), channel_id=1, replica_groups=mesh['dp'=4,'expert'=8] {'expert'}, dimensions={0} | all-to-all | bytes 2097152 | tf_op jit(solution)/shard_map/all_to_all | solution.py:90
  81.5 18.0 %all-gather.3.cloned.1.call-done = bf16[32,1,32,2048]{3,2,1,0:T(8,128)(2,1)} async-done(((bf16[8,1,32,2048]{3,2,1,0:T(8,128)(2,1)}), bf16[32,1,32,2048]{3,2,1,0:T(8,128)(2,1)}) %all-gather.3.cloned.1.call-update) | async-done | bytes 4194320 | tf_op jit(solution)/shard_map/all_gather | solution.py:84
  99.5 6.3 %fusion.8 = f32[32,32,352]{2,1,0:T(8,128)} fusion(bf16[32,1,32,2048]{3,2,1,0:T(8,128)(2,1)} %all-gather.3.cloned.1.call-done, bf16[1,2,352,2048]{3,2,1,0:T(8,128)(2,1)} %param.12), kind=kOutput, calls=%fused_computation.15 | convolution fusion | flops 1476395008 | bytes 7077888 | tf_op jit(solution)/shard_map/gecd,ehd->gech/dot_general | solution.py:11
  105.8 3.5 %fusion.10 = f32[32,32,352]{2,1,0:T(8,128)} fusion(bf16[32,1,32,2048]{3,2,1,0:T(8,128)(2,1)S(1)} %copy-done.10, bf16[1,2,352,2048]{3,2,1,0:T(8,128)(2,1)S(1)} %copy-done.2), kind=kOutput, calls=%fused_computation.17 | convolution fusion | flops 1476395008 | bytes 7077888 | tf_op jit(solution)/shard_map/gecd,ehd->gech/dot_general | solution.py:8
  109.3 44.7 %all-gather.5.cloned.1.call-done = bf16[32,1,32,2048]{3,2,1,0:T(8,128)(2,1)} async-done(((bf16[8,1,32,2048]{3,2,1,0:T(8,128)(2,1)}), bf16[32,1,32,2048]{3,2,1,0:T(8,128)(2,1)}) %all-gather.5.cloned.1.call-update) | async-done | bytes 4194320 | tf_op jit(solution)/shard_map/all_gather | solution.py:91
  154.1 5.9 %fusion.62 = (bf16[32,32,352]{2,1,0:T(8,128)(2,1)S(1)}, bf16[32,1,32,352]{3,2,0,1:T(8,128)(2,1)S(1)}, bf16[32,32,352]{2,1,0:T(8,128)(2,1)S(1)}) fusion(f32[32,32,352]{2,1,0:T(8,128)} %fusion.10, f32[32,32,352]{2,1,0:T(8,128)} %fusion.8, bf16[1,352,2048]{2,1,0:T(8,128)(2,1)S(1)} %copy-done, bf16[32,1,32,2048]{3,2,1,0:T(8,128)(2,1)} %all-gather.5.cloned.1.call-done), kind=kOutput, calls=%fused_computation.62 | convolution fusion | flops 1481801728 | bytes 10682368 | tf_op jit(solution)/shard_map/gecd,ehd->gech/dot_general | solution.py:25
  160.9 4.3 %convert_bitcast_fusion = bf16[32,1,32,2048]{3,2,0,1:T(8,128)(2,1)} fusion(bf16[32,32,352]{2,1,0:T(8,128)(2,1)S(1)} %get-tuple-element.16, bf16[1,352,2048]{2,1,0:T(8,128)(2,1)S(1)} %copy-done), kind=kOutput, calls=%fused_computation.19 | convolution fusion | flops 1478492160 | bytes 6356992 | tf_op jit(solution)/shard_map/gech,ehd->gecd/dot_general | solution.py:17
  165.4 3.8 %fusion.52 = f32[32,32,2048]{2,1,0:T(8,128)S(1)} fusion(bf16[1,2,352,2048]{3,2,1,0:T(8,128)(2,1)} %param.12, bf16[32,1,32,352]{3,2,0,1:T(8,128)(2,1)S(1)} %get-tuple-element.15), kind=kOutput, calls=%fused_computation.52 | convolution fusion | flops 1476395008 | bytes 10551296 | tf_op jit(solution)/shard_map/gech,ehd->gecd/dot_general | solution.py:40
  169.3 4.3 %fusion.12 = bf16[32,1,32,2048]{3,2,0,1:T(8,128)(2,1)} fusion(f32[32,32,2048]{2,1,0:T(8,128)S(1)} %fusion.52, bf16[32,32,352]{2,1,0:T(8,128)(2,1)S(1)} %get-tuple-element.14, bf16[1,2,352,2048]{3,2,1,0:T(8,128)(2,1)S(1)} %copy-done.3), kind=kOutput, calls=%fused_computation.20 | convolution fusion | flops 1480589312 | bytes 14811136 | tf_op jit(solution)/shard_map/gech,ehd->gecd/dot_general | solution.py:43
  175.8 42.2 %reduce-scatter.3.cloned.1.call-done = bf16[8,1,32,2048]{3,2,0,1:T(8,128)(2,1)} async-done(((bf16[32,1,32,2048]{3,2,0,1:T(8,128)(2,1)}), bf16[8,1,32,2048]{3,2,0,1:T(8,128)(2,1)}) %reduce-scatter.3.cloned.1.call-update) | async-done | bytes 1048592 | tf_op jit(solution)/shard_map/reduce_scatter | solution.py:86
  218.0 4.6 %all-to-all-start.1 = ((bf16[8,1,32,2048]{3,2,1,0:T(8,128)(2,1)}), bf16[8,1,32,2048]{3,2,1,0:T(8,128)(2,1)S(1)}, u32[]{:S(2)}, u32[]{:S(2)}) async-start(bf16[8,1,32,2048]{3,2,1,0:T(8,128)(2,1)} %bitcast.187), calls=%async_computation.2 | async-start | bytes 2097152 | tf_op jit(solution)/shard_map/all_to_all | solution.py:89
  222.7 5.1 %fusion.34 = bf16[1,1,352,2048]{3,2,1,0:T(8,128)(2,1)} fusion(bf16[32,32,352]{2,1,0:T(8,128)(2,1)S(1)} %get-tuple-element.14, bf16[32,1,32,2048]{3,2,1,0:T(8,128)(2,1)} %all-gather.3.cloned.1.call-done), kind=kOutput, calls=%fused_computation.29 | convolution fusion | flops 1477115904 | bytes 6356992 | tf_op jit(solution)/shard_map/gech,gecd->ehd/dot_general | solution.py:34
  227.8 2.8 fusion.31
  230.6 43.2 %reduce-scatter.5.cloned.1.call-done = bf16[8,1,32,2048]{3,2,0,1:T(8,128)(2,1)} async-done(((bf16[32,1,32,2048]{3,2,0,1:T(8,128)(2,1)}), bf16[8,1,32,2048]{3,2,0,1:T(8,128)(2,1)}) %reduce-scatter.5.cloned.1.call-update) | async-done | bytes 1048592 | tf_op jit(solution)/shard_map/reduce_scatter | solution.py:95
  273.9 4.6 %all-to-all-start.3 = ((bf16[8,1,32,2048]{3,2,1,0:T(8,128)(2,1)}), bf16[8,1,32,2048]{3,2,1,0:T(8,128)(2,1)}, u32[]{:S(2)}, u32[]{:S(2)}) async-start(bf16[8,1,32,2048]{3,2,1,0:T(8,128)(2,1)} %bitcast.186), calls=%async_computation.5 | async-start | bytes 2097152 | tf_op jit(solution)/shard_map/all_to_all | solution.py:98
  278.5 3.8 %pad_maximum_fusion = bf16[1,2,352,2048]{3,2,1,0:T(8,128)(2,1)} fusion(bf16[1,1,352,2048]{3,2,1,0:T(8,128)(2,1)} %fusion.34, bf16[1,1,352,2048]{3,2,1,0:T(8,128)(2,1)} %fusion.31), kind=kLoop, calls=%fused_computation.24 | loop fusion | flops 1441792 | bytes 5767168 | tf_op jit(solution)/shard_map/stack | solution.py:46
  282.3 2.8 fusion.37
  285.1 1.3 concatenate.25
  286.4 2.3 gather_fusion.1
  288.7 2.4 reshape.229
  291.1 6.0 %multiply_reduce_fusion = (f32[128,2]{1,0:T(8,128)}, bf16[128,2048]{1,0:T(8,128)(2,1)}) fusion(f32[128,2,2048]{2,1,0:T(2,128)S(1)} %reshape.229, f32[128,2048]{1,0:T(8,128)} %convert_element_type.115, f32[128,2]{1,0:T(8,128)} %copy-done.8), kind=kLoop, calls=%fused_computation.33 | loop fusion | flops 1834752 | bytes 3672064 | tf_op jit(solution)/shard_map/reduce_sum | solution.py:108
  297.0 1.5 copy.39
  298.5 6.7 %all-to-all-done.3 = bf16[8,1,32,2048]{3,2,1,0:T(8,128)(2,1)} async-done(((bf16[8,1,32,2048]{3,2,1,0:T(8,128)(2,1)}), bf16[8,1,32,2048]{3,2,1,0:T(8,128)(2,1)}, u32[]{:S(2)}, u32[]{:S(2)}) %all-to-all-start.3) | async-done | bytes 1048608 | tf_op jit(solution)/shard_map/all_to_all | solution.py:98
  305.2 1.3 concatenate.28
  306.5 2.3 gather_fusion.4
  308.8 1.7 reshape.228
  310.5 3.6 %reduce_sum.57 = bf16[128,2048]{1,0:T(8,128)(2,1)} reduce(bf16[128,2,2048]{2,1,0:T(2,128)(2,1)S(1)} %reshape.228, bf16[]{:T(256)} %constant.14.clone.1), dimensions={1}, to_apply=%region_8.9 | reduce | flops 262144 | bytes 1572866 | tf_op jit(solution)/shard_map/reduce_sum | solution.py:109
  (64 shorter events, 8.9 us)
Async XLA Ops:
  7.2 146.9 %copy-start = (bf16[1,352,2048]{2,1,0:T(8,128)(2,1)S(1)}, bf16[1,352,2048]{2,1,0:T(8,128)(2,1)}, u32[]{:S(2)}) copy-start(bf16[1,352,2048]{2,1,0:T(8,128)(2,1)} %param.13) | copy-start | bytes 4325380
  7.2 92.3 %all-gather.3.cloned.1.call-start = ((), (), s32[]{:S(2)}) async-start(), calls=%async_computation.6 | async-start | bytes 5242880 | tf_op jit(solution)/shard_map/all_gather | solution.py:84
  14.9 32.9 %copy-start.9 = (f32[128,2]{0,1:T(2,128)S(1)}, f32[128,2]{0,1:T(2,128)}, u32[]{:S(2)}) copy-start(f32[128,2]{0,1:T(2,128)} %param.10) | copy-start | bytes 3076
  47.7 2.4 copy-start.4
  47.7 106.3 %all-gather.5.cloned.1.call-start = ((), (), s32[]{:S(2)}) async-start(), calls=%async_computation.8 | async-start | bytes 5242880 | tf_op jit(solution)/shard_map/all_gather | solution.py:91
  47.9 2.2 copy-start.8
  81.5 136.5 %reduce-scatter.3.cloned.1.call-start = ((), (), s32[]{:S(2)}) async-start(), calls=%async_computation.7 | async-start | bytes 5242880 | tf_op jit(solution)/shard_map/reduce_scatter | solution.py:86
  99.5 6.3 %copy-start.2 = (bf16[1,2,352,2048]{3,2,1,0:T(8,128)(2,1)S(1)}, bf16[1,2,352,2048]{3,2,1,0:T(8,128)(2,1)}, u32[]{:S(2)}) copy-start(bf16[1,2,352,2048]{3,2,1,0:T(8,128)(2,1)} %param.12) | copy-start | bytes 8650756
  99.5 6.3 %copy-start.10 = (bf16[32,1,32,2048]{3,2,1,0:T(8,128)(2,1)S(1)}, bf16[32,1,32,2048]{3,2,1,0:T(8,128)(2,1)}, u32[]{:S(2)}) copy-start(bf16[32,1,32,2048]{3,2,1,0:T(8,128)(2,1)} %all-gather.3.cloned.1.call-done) | copy-start | bytes 12582916
  160.0 0.9 copy-start.13
  160.0 5.4 %copy-start.6 = (bf16[32,1,32,352]{3,2,0,1:T(8,128)(2,1)}, bf16[32,1,32,352]{3,2,0,1:T(8,128)(2,1)S(1)}, u32[]{:S(2)}) copy-start(bf16[32,1,32,352]{3,2,0,1:T(8,128)(2,1)S(1)} %get-tuple-element.15) | copy-start | bytes 2162692
  165.2 108.7 %reduce-scatter.5.cloned.1.call-start = ((), (), s32[]{:S(2)}) async-start(), calls=%async_computation.9 | async-start | bytes 5242880 | tf_op jit(solution)/shard_map/reduce_scatter | solution.py:95
  165.4 3.9 %copy-start.3 = (bf16[1,2,352,2048]{3,2,1,0:T(8,128)(2,1)S(1)}, bf16[1,2,352,2048]{3,2,1,0:T(8,128)(2,1)}, u32[]{:S(2)}) copy-start(bf16[1,2,352,2048]{3,2,1,0:T(8,128)(2,1)} %param.12) | copy-start | bytes 8650756
  173.6 1.0 copy-start.5
  218.0 55.8 %all-to-all-start.1 = ((bf16[8,1,32,2048]{3,2,1,0:T(8,128)(2,1)}), bf16[8,1,32,2048]{3,2,1,0:T(8,128)(2,1)S(1)}, u32[]{:S(2)}, u32[]{:S(2)}) async-start(bf16[8,1,32,2048]{3,2,1,0:T(8,128)(2,1)} %bitcast.187), calls=%async_computation.2 | async-start | bytes 2097152 | tf_op jit(solution)/shard_map/all_to_all | solution.py:89
  222.6 5.1 %copy-start.7 = (bf16[32,1,32,352]{3,2,0,1:T(8,128)(2,1)S(1)}, bf16[32,1,32,352]{3,2,0,1:T(8,128)(2,1)}, u32[]{:S(2)}) copy-start(bf16[32,1,32,352]{3,2,0,1:T(8,128)(2,1)} %copy-done.6) | copy-start | bytes 2162692
  222.7 5.1 %copy-start.11 = (bf16[32,1,32,2048]{3,2,1,0:T(8,128)(2,1)S(1)}, bf16[32,1,32,2048]{3,2,1,0:T(8,128)(2,1)}, u32[]{:S(2)}) copy-start(bf16[32,1,32,2048]{3,2,1,0:T(8,128)(2,1)} %all-gather.3.cloned.1.call-done) | copy-start | bytes 12582916
  273.9 8.4 %copy-start.1 = (bf16[8,1,32,2048]{3,2,1,0:T(8,128)(2,1)}, bf16[8,1,32,2048]{3,2,1,0:T(8,128)(2,1)S(1)}, u32[]{:S(2)}) copy-start(bf16[8,1,32,2048]{3,2,1,0:T(8,128)(2,1)S(1)} %all-to-all-done.1) | copy-start | bytes 3145732
  273.9 31.3 %all-to-all-start.3 = ((bf16[8,1,32,2048]{3,2,1,0:T(8,128)(2,1)}), bf16[8,1,32,2048]{3,2,1,0:T(8,128)(2,1)}, u32[]{:S(2)}, u32[]{:S(2)}) async-start(bf16[8,1,32,2048]{3,2,1,0:T(8,128)(2,1)} %bitcast.186), calls=%async_computation.5 | async-start | bytes 2097152 | tf_op jit(solution)/shard_map/all_to_all | solution.py:98
  278.5 3.8 %copy-start.12 = (bf16[32,1,32,2048]{3,2,1,0:T(8,128)(2,1)S(1)}, bf16[32,1,32,2048]{3,2,1,0:T(8,128)(2,1)}, u32[]{:S(2)}) copy-start(bf16[32,1,32,2048]{3,2,1,0:T(8,128)(2,1)} %all-gather.5.cloned.1.call-done) | copy-start | bytes 12582916
  278.5 3.8 %copy-start.14 = (bf16[32,32,352]{2,1,0:T(8,128)(2,1)S(1)}, bf16[32,32,352]{2,1,0:T(8,128)(2,1)}, u32[]{:S(2)}) copy-start(bf16[32,32,352]{2,1,0:T(8,128)(2,1)} %copy-done.13) | copy-start | bytes 2162692
Sparse Core Ops, SparseCore 0:
  47.8 51.5 all-gather.2
  101.3 52.6 all-gather.4
  165.3 52.6 reduce-scatter.2
  221.1 52.6 reduce-scatter.4
where the time goes:
time: 321 us
  waiting for transfers between devices  155 us (48%)
  blocking collectives  62.5 us (19%)
  matrix products  39 us (12%)
  local copies, waits for them, and re-layouts  23.8 us (7%)
  other arithmetic  16.9 us (5%)
  between operations  14 us (4%)
  starting transfers between devices  9.58 us (3%)
    all_gather x1, waiting for transfers between devices, body(): use_scaled = lax.all_gather(recv_scaled, 'dp', axis=0, tiled=True)  44.7 us
    reduce_scatter x1, waiting for transfers between devices, body(): lax.psum_scatter(input_grad.astype(jnp.bfloat16), 'dp', scatter_dimension...  43.2 us
    reduce_scatter x1, waiting for transfers between devices, body(): lax.psum_scatter(partial_out.astype(jnp.bfloat16), 'dp', scatter_dimensio...  42.2 us
    all_to_all x1, blocking collectives, body(): lax.all_to_all(send_inputs, 'expert', split_axis=0, concat_axis=0, tiled=...  32.8 us
    all_to_all x1, blocking collectives, body(): lax.all_to_all(send_scaled, 'expert', split_axis=0, concat_axis=0, tiled=...  29.7 us
    all_gather x1, waiting for transfers between devices, body(): use_inputs = lax.all_gather(recv_inputs, 'dp', axis=0, tiled=True)  18 us
    all_to_all x1, waiting for transfers between devices, body(): lax.all_to_all(grad_local, 'expert', split_axis=0, concat_axis=0, tiled=T...  6.66 us
  transfers between devices with their start and end apart: 6, of which 5 were waited for; matrix products, arithmetic and copies ran while one was open for 16% of the time, Pallas kernels for 0%

commit v1 on v0

--- a/solution.py
+++ b/solution.py
@@ -2,6 +2,16 @@
 import jax.numpy as jnp
 from jax import lax
 from jax.sharding import PartitionSpec as P
+
+
+def gather_by_hops(block, name, d):
+    size = lax.axis_size(name)
+    held, blocks = (block, [block])
+    for _ in range(size - 1):
+        held = lax.ppermute(held, name, [(i, (i + 1) % size) for i in range(size)])
+        blocks.insert(0, held)
+    line = jnp.concatenate(blocks, axis=d)
+    return jnp.roll(line, (lax.axis_index(name) + 1) * block.shape[d], axis=d)
 
 
 def expert_forward(inputs, weights_in, weights_down):
@@ -88,7 +98,7 @@
     )
     out_back = lax.all_to_all(out_local, "expert", split_axis=0, concat_axis=0, tiled=True)
     recv_scaled = lax.all_to_all(send_scaled, "expert", split_axis=0, concat_axis=0, tiled=True)
-    use_scaled = lax.all_gather(recv_scaled, "dp", axis=0, tiled=True)
+    use_scaled = gather_by_hops(recv_scaled, "dp", 0)
     in_weight_grad, down_weight_grad, input_grad = expert_backward(
         use_inputs, use_scaled, w_in, w_down, saved
     )

time: 321 us -> 367 us (1.14)
  waiting for transfers between devices: 155 us -> 241 us
  blocking collectives: 62.5 us -> 0 us
  starting transfers between devices: 9.58 us -> 23.3 us
  local copies, waits for them, and re-layouts: 23.8 us -> 35 us
    ppermute x0 -> x3, waiting for transfers between devices: none -> 91.2 us  [gather_by_hops(): held = lax.ppermute(held, name, [(i, (i + 1) % size) for i in range(size)])]
    all_to_all x2 -> x0, blocking collectives: 62.5 us -> none  [the longest x1 32.8 us: body(): lax.all_to_all(send_inputs, 'expert', split_axis=0, concat_axis=0, tiled=...]
    all_to_all x0 -> x2, waiting for transfers between devices: none -> 45.8 us  [the longest x1 25.7 us: body(): lax.all_to_all(send_scaled, 'expert', split_axis=0, concat_axis=0, tiled=...]
    all_gather x1 -> x0, waiting for transfers between devices: 44.7 us -> none  [body(): use_scaled = lax.all_gather(recv_scaled, 'dp', axis=0, tiled=True)]
    all_gather x1, waiting for transfers between devices: 18 us -> 0.01 us  [body(): use_inputs = lax.all_gather(recv_inputs, 'dp', axis=0, tiled=True)]
    unnamed x33 -> x32, local copies, waits for them, and re-layouts: 4.31 us -> 15.6 us
    all_to_all x1, waiting for transfers between devices: 0.01 us -> 9.97 us  [body(): lax.all_to_all(out_local, 'expert', split_axis=0, concat_axis=0, tiled=True)]
    all_to_all x0 -> x2, starting transfers between devices: none -> 9.88 us  [the longest x1 6.33 us: body(): lax.all_to_all(send_inputs, 'expert', split_axis=0, concat_axis=0, tiled=...]
  transfers between devices with their start and end apart: 6 -> 10, of which waited for: 5 -> 8; matrix products, arithmetic and copies ran while one was open for 16% -> 12% of each run, Pallas kernels for 0% -> 0%
where the time goes in v1:
time: 367 us; the launch traced here: 366 us
  waiting for transfers between devices  241 us (66%)
  matrix products  36.6 us (10%)
  local copies, waits for them, and re-layouts  35 us (10%)
  starting transfers between devices  23.3 us (6%)
  other arithmetic  15.8 us (4%)
  between operations  14 us (4%)
    ppermute x3, waiting for transfers between devices, gather_by_hops(): held = lax.ppermute(held, name, [(i, (i + 1) % size) for i in range(size)])  91.2 us
    reduce_scatter x1, waiting for transfers between devices, body(): lax.psum_scatter(input_grad.astype(jnp.bfloat16), 'dp', scatter_dimension...  47.4 us
    reduce_scatter x1, waiting for transfers between devices, body(): lax.psum_scatter(partial_out.astype(jnp.bfloat16), 'dp', scatter_dimensio...  46.2 us
    all_to_all x1, waiting for transfers between devices, body(): lax.all_to_all(send_scaled, 'expert', split_axis=0, concat_axis=0, tiled=...  25.7 us
    all_to_all x1, waiting for transfers between devices, body(): lax.all_to_all(send_inputs, 'expert', split_axis=0, concat_axis=0, tiled=...  20.1 us
    unnamed x32, local copies, waits for them, and re-layouts  15.6 us
    all_to_all x1, waiting for transfers between devices, body(): lax.all_to_all(out_local, 'expert', split_axis=0, concat_axis=0, tiled=True)  9.97 us
  transfers between devices with their start and end apart: 10, of which 8 were waited for; matrix products, arithmetic and copies ran while one was open for 12% of the time, Pallas kernels for 0%

profile of v1, /device:TPU:0, one launch (start us, length us, event | category | flops | bytes accessed | tf_op | source)
XLA Modules:
  0.0 366.1 jit_solution(636159580850233496)
XLA Ops:
  13.4 2.3 gather_fusion
  15.8 6.3 %all-to-all-start = ((bf16[8,1,32,2048]{3,2,1,0:T(8,128)(2,1)}), bf16[8,1,32,2048]{3,2,1,0:T(8,128)(2,1)}, u32[]{:S(2)}, u32[]{:S(2)}) async-start(bf16[8,1,32,2048]{3,2,1,0:T(8,128)(2,1)} %bitcast.6), calls=%async_computation | async-start | bytes 2097152 | tf_op jit(solution)/shard_map/all_to_all | solution.py:93
  25.5 1.9 gather_fusion.2
  28.7 20.1 %all-to-all-done = bf16[8,1,32,2048]{3,2,1,0:T(8,128)(2,1)} async-done(((bf16[8,1,32,2048]{3,2,1,0:T(8,128)(2,1)}), bf16[8,1,32,2048]{3,2,1,0:T(8,128)(2,1)}, u32[]{:S(2)}, u32[]{:S(2)}) %all-to-all-start) | async-done | bytes 1048608 | tf_op jit(solution)/shard_map/all_to_all | solution.py:93
  48.8 3.6 all-to-all-start.2
  53.1 25.7 %all-to-all-done.2 = bf16[8,1,32,2048]{3,2,1,0:T(8,128)(2,1)S(1)} async-done(((bf16[8,1,32,2048]{3,2,1,0:T(8,128)(2,1)}), bf16[8,1,32,2048]{3,2,1,0:T(8,128)(2,1)S(1)}, u32[]{:S(2)}, u32[]{:S(2)}) %all-to-all-start.2) | async-done | bytes 1048608 | tf_op jit(solution)/shard_map/all_to_all | solution.py:100
  80.4 42.7 %collective-permute-done = bf16[8,1,32,2048]{3,2,1,0:T(8,128)(2,1)S(1)} collective-permute-done((bf16[8,1,32,2048]{3,2,1,0:T(8,128)(2,1)S(1)}, bf16[8,1,32,2048]{3,2,1,0:T(8,128)(2,1)S(1)}, u32[]{:S(2)}, u32[]{:S(2)}) %collective-permute-start) | collective-permute-done | bytes 1048608 | tf_op jit(solution)/shard_map/ppermute | solution.py:11
  123.1 2.0 collective-permute-start.1
  125.1 24.4 %collective-permute-done.1 = bf16[8,1,32,2048]{3,2,1,0:T(8,128)(2,1)} collective-permute-done((bf16[8,1,32,2048]{3,2,1,0:T(8,128)(2,1)S(1)}, bf16[8,1,32,2048]{3,2,1,0:T(8,128)(2,1)}, u32[]{:S(2)}, u32[]{:S(2)}) %collective-permute-start.1) | collective-permute-done | bytes 1048608 | tf_op jit(solution)/shard_map/ppermute | solution.py:11
  150.1 24.1 %collective-permute-done.2 = bf16[8,1,32,2048]{3,2,1,0:T(8,128)(2,1)} collective-permute-done((bf16[8,1,32,2048]{3,2,1,0:T(8,128)(2,1)}, bf16[8,1,32,2048]{3,2,1,0:T(8,128)(2,1)}, u32[]{:S(2)}, u32[]{:S(2)}) %collective-permute-start.2) | collective-permute-done | bytes 1048608 | tf_op jit(solution)/shard_map/ppermute | solution.py:11
  174.2 2.3 constant_dynamic-update-slice_fusion.7
  176.5 2.3 constant_dynamic-update-slice_fusion.6
  181.0 2.3 constant_dynamic-update-slice_fusion.3
  183.3 2.3 constant_dynamic-update-slice_fusion.2
  187.8 5.1 %fusion.10 = f32[32,32,352]{2,1,0:T(8,128)S(1)} fusion(bf16[32,1,32,2048]{3,2,1,0:T(8,128)(2,1)} %all-gather.2.cloned.1.call-done, bf16[1,2,352,2048]{3,2,1,0:T(8,128)(2,1)} %param.12), kind=kOutput, calls=%fused_computation.17 | convolution fusion | flops 1476395008 | bytes 7077888 | tf_op jit(solution)/shard_map/gecd,ehd->gech/dot_general | solution.py:18
  192.9 2.3 fusion.8
  195.3 5.1 %fusion.64 = (bf16[32,32,352]{2,1,0:T(8,128)(2,1)S(1)}, bf16[32,1,32,352]{3,2,0,1:T(8,128)(2,1)S(1)}, bf16[32,32,352]{2,1,0:T(8,128)(2,1)S(1)}) fusion(f32[32,32,352]{2,1,0:T(8,128)S(1)} %fusion.10, f32[32,32,352]{2,1,0:T(8,128)S(1)} %fusion.8, bf16[1,352,2048]{2,1,0:T(8,128)(2,1)S(1)} %copy-done, ...), kind=kOutput, calls=%fused_computation.64 | convolution fusion | flops 1481801728 | bytes 10682372 | tf_op jit(solution)/shard_map/gecd,ehd->gech/dot_general | solution.py:35
  200.4 2.3 fusion.54
  202.8 4.3 %fusion.14 = bf16[32,1,32,2048]{3,2,0,1:T(8,128)(2,1)} fusion(f32[32,32,2048]{2,1,0:T(8,128)S(1)} %fusion.54, bf16[32,32,352]{2,1,0:T(8,128)(2,1)S(1)} %get-tuple-element.14, bf16[1,2,352,2048]{3,2,1,0:T(8,128)(2,1)S(1)} %copy-done.2), kind=kOutput, calls=%fused_computation.22 | convolution fusion | flops 1480589312 | bytes 14811136 | tf_op jit(solution)/shard_map/gech,ehd->gecd/dot_general | solution.py:53
  207.1 4.3 %convert_bitcast_fusion = bf16[32,1,32,2048]{3,2,0,1:T(8,128)(2,1)} fusion(bf16[32,32,352]{2,1,0:T(8,128)(2,1)S(1)} %get-tuple-element.16, bf16[1,352,2048]{2,1,0:T(8,128)(2,1)S(1)} %copy-done), kind=kOutput, calls=%fused_computation.19 | convolution fusion | flops 1478492160 | bytes 6356992 | tf_op jit(solution)/shard_map/gech,ehd->gecd/dot_general | solution.py:27
  211.4 47.4 %reduce-scatter.5.cloned.1.call-done = bf16[8,1,32,2048]{3,2,0,1:T(8,128)(2,1)} async-done(((bf16[32,1,32,2048]{3,2,0,1:T(8,128)(2,1)}), bf16[8,1,32,2048]{3,2,0,1:T(8,128)(2,1)}) %reduce-scatter.5.cloned.1.call-update) | async-done | bytes 1048592 | tf_op jit(solution)/shard_map/reduce_scatter | solution.py:105
  258.8 4.6 %all-to-all-start.3 = ((bf16[8,1,32,2048]{3,2,1,0:T(8,128)(2,1)}), bf16[8,1,32,2048]{3,2,1,0:T(8,128)(2,1)S(1)}, u32[]{:S(2)}, u32[]{:S(2)}) async-start(bf16[8,1,32,2048]{3,2,1,0:T(8,128)(2,1)} %bitcast.185), calls=%async_computation.5 | async-start | bytes 2097152 | tf_op jit(solution)/shard_map/all_to_all | solution.py:108
  264.5 4.1 %fusion.36 = bf16[1,1,352,2048]{3,2,1,0:T(8,128)(2,1)S(1)} fusion(bf16[32,1,32,2048]{3,2,1,0:T(8,128)(2,1)} %all-gather.2.cloned.1.call-done, bf16[32,1,32,352]{3,2,0,1:T(8,128)(2,1)} %copy-done.5), kind=kOutput, calls=%fused_computation.31 | convolution fusion | flops 1477115904 | bytes 6356992 | tf_op jit(solution)/shard_map/gech,gecd->ehd/dot_general | solution.py:41
  268.6 46.2 %reduce-scatter.3.cloned.1.call-done = bf16[8,1,32,2048]{3,2,0,1:T(8,128)(2,1)} async-done(((bf16[32,1,32,2048]{3,2,0,1:T(8,128)(2,1)}), bf16[8,1,32,2048]{3,2,0,1:T(8,128)(2,1)}) %reduce-scatter.3.cloned.1.call-update) | async-done | bytes 1048592 | tf_op jit(solution)/shard_map/reduce_scatter | solution.py:96
  314.8 4.6 %all-to-all-start.1 = ((bf16[8,1,32,2048]{3,2,1,0:T(8,128)(2,1)}), bf16[8,1,32,2048]{3,2,1,0:T(8,128)(2,1)}, u32[]{:S(2)}, u32[]{:S(2)}) async-start(bf16[8,1,32,2048]{3,2,1,0:T(8,128)(2,1)} %bitcast.184), calls=%async_computation.2 | async-start | bytes 2097152 | tf_op jit(solution)/shard_map/all_to_all | solution.py:99
  319.4 4.1 %fusion.39 = bf16[1,1,352,2048]{3,2,1,0:T(8,128)(2,1)S(1)} fusion(bf16[32,32,352]{2,1,0:T(8,128)(2,1)} %copy-done.4, bf16[32,1,32,2048]{3,2,1,0:T(8,128)(2,1)} %all-gather.2.cloned.1.call-done), kind=kOutput, calls=%fused_computation.32 | convolution fusion | flops 1477115904 | bytes 6356992 | tf_op jit(solution)/shard_map/gech,gecd->ehd/dot_general | solution.py:44
  325.3 5.0 %fusion.33 = bf16[1,352,2048]{2,1,0:T(8,128)(2,1)} fusion(bf16[32,32,352]{2,1,0:T(8,128)(2,1)S(1)} %copy-done.10, bf16[64,1,32,2048]{3,2,1,0:T(8,128)(2,1)} %constant_dynamic-update-slice_fusion, s32[]{:T(128)S(6)} %select_n.54), kind=kOutput, calls=%fused_computation.30 | convolution fusion | flops 1477115904 | bytes 6356996 | tf_op jit(solution)/shard_map/gech,gecd->ehd/dot_general | solution.py:47
  332.5 3.6 reduce_sum.57
  336.1 10.0 %all-to-all-done.1 = bf16[8,1,32,2048]{3,2,1,0:T(8,128)(2,1)} async-done(((bf16[8,1,32,2048]{3,2,1,0:T(8,128)(2,1)}), bf16[8,1,32,2048]{3,2,1,0:T(8,128)(2,1)}, u32[]{:S(2)}, u32[]{:S(2)}) %all-to-all-start.1) | async-done | bytes 1048608 | tf_op jit(solution)/shard_map/all_to_all | solution.py:99
  347.4 2.3 gather_fusion.1
  349.7 2.4 reshape.229
  352.1 6.0 %multiply_reduce_fusion = (f32[128,2]{1,0:T(8,128)}, bf16[128,2048]{1,0:T(8,128)(2,1)}) fusion(f32[128,2,2048]{2,1,0:T(2,128)S(1)} %reshape.229, f32[128,2048]{1,0:T(8,128)} %convert_element_type.115, f32[128,2]{1,0:T(8,128)} %copy-done.6), kind=kLoop, calls=%fused_computation.35 | loop fusion | flops 1834752 | bytes 3672064 | tf_op jit(solution)/shard_map/reduce_sum | solution.py:118
  (69 shorter events, 25.9 us)
Async XLA Ops:
  7.2 188.1 %copy-start = (bf16[1,352,2048]{2,1,0:T(8,128)(2,1)S(1)}, bf16[1,352,2048]{2,1,0:T(8,128)(2,1)}, u32[]{:S(2)}) copy-start(bf16[1,352,2048]{2,1,0:T(8,128)(2,1)} %param.13) | copy-start | bytes 4325380
  15.8 33.0 %all-to-all-start = ((bf16[8,1,32,2048]{3,2,1,0:T(8,128)(2,1)}), bf16[8,1,32,2048]{3,2,1,0:T(8,128)(2,1)}, u32[]{:S(2)}, u32[]{:S(2)}) async-start(bf16[8,1,32,2048]{3,2,1,0:T(8,128)(2,1)} %bitcast.6), calls=%async_computation | async-start | bytes 2097152 | tf_op jit(solution)/shard_map/all_to_all | solution.py:93
  23.2 1.4 copy-start.7
  24.7 0.6 copy-start.6
  48.8 30.1 %all-to-all-start.2 = ((bf16[8,1,32,2048]{3,2,1,0:T(8,128)(2,1)}), bf16[8,1,32,2048]{3,2,1,0:T(8,128)(2,1)S(1)}, u32[]{:S(2)}, u32[]{:S(2)}) async-start(bf16[8,1,32,2048]{3,2,1,0:T(8,128)(2,1)} %fusion.42), calls=%async_computation.3 | async-start | bytes 2097152 | tf_op jit(solution)/shard_map/all_to_all | solution.py:100
  52.4 135.4 %all-gather.2.cloned.1.call-start = ((), (), s32[]{:S(2)}) async-start(), calls=%async_computation.6 | async-start | bytes 5242880 | tf_op jit(solution)/shard_map/all_gather | solution.py:94
  53.1 205.7 %reduce-scatter.5.cloned.1.call-start = ((), (), s32[]{:S(2)}) async-start(), calls=%async_computation.8 | async-start | bytes 5242880 | tf_op jit(solution)/shard_map/reduce_scatter | solution.py:105
  78.9 44.2 %collective-permute-start = (bf16[8,1,32,2048]{3,2,1,0:T(8,128)(2,1)S(1)}, bf16[8,1,32,2048]{3,2,1,0:T(8,128)(2,1)S(1)}, u32[]{:S(2)}, u32[]{:S(2)}) collective-permute-start(bf16[8,1,32,2048]{3,2,1,0:T(8,128)(2,1)S(1)} %all-to-all-done.2), channel_id=1, source_target_pairs={{0,8},{8,16},{16,24},{24,0},{1,9},{9,17},{17,25},{25,1},{2,10},{10... | collective-permute-start | bytes 3145736 | tf_op jit(solution)/shard_map/ppermute | solution.py:11
  123.1 26.4 %collective-permute-start.1 = (bf16[8,1,32,2048]{3,2,1,0:T(8,128)(2,1)S(1)}, bf16[8,1,32,2048]{3,2,1,0:T(8,128)(2,1)}, u32[]{:S(2)}, u32[]{:S(2)}) collective-permute-start(bf16[8,1,32,2048]{3,2,1,0:T(8,128)(2,1)S(1)} %collective-permute-done), channel_id=1, source_target_pairs={{0,8},{8,16},{16,24},{24,0},{1,9},{9,17},{17,25},{25,1},{2,10},{10... | collective-permute-start | bytes 3145736 | tf_op jit(solution)/shard_map/ppermute | solution.py:11
  149.5 24.7 %collective-permute-start.2 = (bf16[8,1,32,2048]{3,2,1,0:T(8,128)(2,1)}, bf16[8,1,32,2048]{3,2,1,0:T(8,128)(2,1)}, u32[]{:S(2)}, u32[]{:S(2)}) collective-permute-start(bf16[8,1,32,2048]{3,2,1,0:T(8,128)(2,1)} %collective-permute-done.1), channel_id=1, source_target_pairs={{0,8},{8,16},{16,24},{24,0},{1,9},{9,17},{17,25},{25,1},{2,10},{10... | collective-permute-start | bytes 3145736 | tf_op jit(solution)/shard_map/ppermute | solution.py:11
  187.8 5.1 %copy-start.2 = (bf16[1,2,352,2048]{3,2,1,0:T(8,128)(2,1)S(1)}, bf16[1,2,352,2048]{3,2,1,0:T(8,128)(2,1)}, u32[]{:S(2)}) copy-start(bf16[1,2,352,2048]{3,2,1,0:T(8,128)(2,1)} %param.12) | copy-start | bytes 8650756
  187.8 5.1 %copy-start.8 = (bf16[32,1,32,2048]{3,2,1,0:T(8,128)(2,1)S(1)}, bf16[32,1,32,2048]{3,2,1,0:T(8,128)(2,1)}, u32[]{:S(2)}) copy-start(bf16[32,1,32,2048]{3,2,1,0:T(8,128)(2,1)} %all-gather.2.cloned.1.call-done) | copy-start | bytes 12582916
  200.4 2.4 copy-start.5
  200.4 2.4 copy-start.4
  200.4 6.7 %copy-start.9 = (bf16[32,32,352]{2,1,0:T(8,128)(2,1)}, bf16[32,32,352]{2,1,0:T(8,128)(2,1)S(1)}, u32[]{:S(2)}) copy-start(bf16[32,32,352]{2,1,0:T(8,128)(2,1)S(1)} %get-tuple-element.16) | copy-start | bytes 2162692
  207.1 107.7 %reduce-scatter.3.cloned.1.call-start = ((), (), s32[]{:S(2)}) async-start(), calls=%async_computation.7 | async-start | bytes 5242880 | tf_op jit(solution)/shard_map/reduce_scatter | solution.py:96
  211.4 52.0 %copy-start.3 = (bf16[128,2048]{1,0:T(8,128)(2,1)S(1)}, bf16[128,2048]{1,0:T(8,128)(2,1)}, u32[]{:S(2)}) copy-start(bf16[128,2048]{1,0:T(8,128)(2,1)} %param.8) | copy-start | bytes 1572868
  258.8 56.0 %all-to-all-start.3 = ((bf16[8,1,32,2048]{3,2,1,0:T(8,128)(2,1)}), bf16[8,1,32,2048]{3,2,1,0:T(8,128)(2,1)S(1)}, u32[]{:S(2)}, u32[]{:S(2)}) async-start(bf16[8,1,32,2048]{3,2,1,0:T(8,128)(2,1)} %bitcast.185), calls=%async_computation.5 | async-start | bytes 2097152 | tf_op jit(solution)/shard_map/all_to_all | solution.py:108
  314.8 31.3 %all-to-all-start.1 = ((bf16[8,1,32,2048]{3,2,1,0:T(8,128)(2,1)}), bf16[8,1,32,2048]{3,2,1,0:T(8,128)(2,1)}, u32[]{:S(2)}, u32[]{:S(2)}) async-start(bf16[8,1,32,2048]{3,2,1,0:T(8,128)(2,1)} %bitcast.184), calls=%async_computation.2 | async-start | bytes 2097152 | tf_op jit(solution)/shard_map/all_to_all | solution.py:99
  323.5 1.8 copy-start.10
  347.4 12.1 %copy-start.1 = (bf16[1,352,2048]{2,1,0:T(8,128)(2,1)S(1)}, bf16[1,352,2048]{2,1,0:T(8,128)(2,1)}, u32[]{:S(2)}) copy-start(bf16[1,352,2048]{2,1,0:T(8,128)(2,1)} %param.13) | copy-start | bytes 4325380
Sparse Core Ops, SparseCore 0:
  55.0 74.9 all-gather.1
  207.2 51.5 reduce-scatter.4
  262.1 52.6 reduce-scatter.2
